TPU v7x, 128 devices: a whole 4x4x4 slice. The times are simulated.
128 devices in a mesh: row: 8 (over x, y_hi), col: 16 (over y_lo, z, core).
Axes of the slice: x: 4, y: 4 (y_hi: 2, y_lo: 2; y = y_hi * 2 + y_lo), z: 4, core: 2. Of those that a mesh axis runs over, the one named last changes fastest.
Arguments:
- values: bfloat16 [8192, 8192], P('row', 'col'), as said below
- pattern: int32 [64, 64], P('row', 'col'), may hold values from 0 to 1, as said below
- filter_mask: int32 [64, 64], P('row', 'col'), may hold values 0 or 1
- assignment: int32 [64], replicated, may hold values from 0 to 63, as said below
Outputs:
- product: bfloat16 [8192, 8192], P('row', 'col')
- occupation: float32 [], replicated
Inputs may be any that keep to these rules, and one draw needn't show every extreme that they name: `assignment`: each block index appears once. The block pattern of P is symmetric: pattern[a, b] equals pattern[c, assignment[a]] where assignment[c] = b; every block row and every block column of pattern holds at most 6 occupied blocks, and some row and some column hold exactly 6; the diagonal blocks of P are occupied. `values`: P is symmetric: entry (i, j) of P equals entry (j, i).
All inputs are finite; a program needn't handle non-finite values. No bound on the sum of `filter_mask` on one device may be relied on, other than what follows from the above.
Results may differ from a plain program's by a relative error of at most 0.0012.
Values may be sent and summed in bfloat16 or wider, within the bound.
A program may use at most 128 MiB of HBM per device.

v0:
```python
import jax
import jax.numpy as jnp
from jax import lax
from jax.sharding import PartitionSpec as P


def on_device(values, pattern, filter_mask, assignment):
    row_blocks = pattern.shape[0]
    col_blocks = pattern.shape[1]
    block_size = values.shape[0] // row_blocks
    all_blocks = assignment.shape[0]
    blocks = values.reshape(row_blocks, block_size, col_blocks, block_size)
    masked_four = blocks * pattern[:, None, :, None].astype(jnp.bfloat16)
    masked = masked_four.reshape(values.shape)
    stacked = lax.all_gather(masked, "row", axis=0, tiled=True)
    inverse = (
        jnp.zeros((all_blocks,), jnp.int32)
        .at[assignment]
        .set(jnp.arange(all_blocks, dtype=jnp.int32))
    )
    natural = jnp.take(stacked.reshape(all_blocks, block_size, -1), inverse, axis=0).reshape(
        stacked.shape
    )
    product = jnp.dot(
        lax.all_gather(masked, "col", axis=1, tiled=True),
        natural,
        preferred_element_type=jnp.float32,
    )
    row_first = lax.axis_index("row") * row_blocks
    global_rows = row_first + jnp.arange(row_blocks, dtype=jnp.int32)
    targets = (
        jnp.take(assignment, global_rows)[:, None] * block_size
        + jnp.arange(block_size, dtype=jnp.int32)[None, :]
    ).reshape(-1)
    columns = lax.axis_index("col") * (col_blocks * block_size) + jnp.arange(
        col_blocks * block_size, dtype=jnp.int32
    )
    partial_trace = jnp.sum(jnp.where(targets[:, None] == columns[None, :], product, 0.0))
    occupation = lax.psum(partial_trace, ("row", "col"))
    kept = product.reshape(row_blocks, block_size, col_blocks, block_size) * filter_mask[
        :, None, :, None
    ].astype(jnp.float32)
    return (kept.reshape(values.shape).astype(jnp.bfloat16), occupation)


def solution(mesh):
    in_specs = (P("row", "col"), P("row", "col"), P("row", "col"), P())
    out_specs = (P("row", "col"), P())
    return jax.shard_map(
        on_device, mesh=mesh, in_specs=in_specs, out_specs=out_specs, check_vma=False
    )
```

profile of v0, /device:TPU:1, one launch (start us, length us, event | category | flops | bytes accessed | tf_op | source)
XLA Modules:
  0.0 304.6 jit_solution(17026182428502971986)
XLA Ops:
  7.2 0.0 all-gather.5.cloned.1.call-start
  7.2 0.7 convert_element_type.11
  7.9 0.1 copy.8
  8.0 0.3 mul.36
  8.3 2.3 bitcast_multiply_fusion.1
  10.7 0.0 all-gather.5.cloned.1.call-update
  10.7 0.0 all-gather.3.cloned.1.call-start
  10.8 0.7 all-gather.3.cloned.1.call-update
  11.5 0.7 convert_element_type.12
  12.2 0.1 copy.9
  12.3 1.3 gather_fusion.1
  13.5 0.7 compare_select_fusion.3
  14.2 0.8 scatter_custom_fusion
  15.1 0.1 add_bitcast_fusion
  15.1 0.1 broadcast_bitcast_fusion
  15.2 107.4 %all-gather.5.cloned.1.call-done = bf16[8192,512]{1,0:T(8,128)(2,1)} async-done(((bf16[1024,512]{1,0:T(8,128)(2,1)}), bf16[8192,512]{1,0:T(8,128)(2,1)}) %all-gather.5.cloned.1.call-update) | async-done | bytes 8388624 | tf_op jit(solution)/shard_map/all_gather | solution.py:15
  122.6 8.9 %gather_fusion = bf16[64,128,512]{2,1,0:T(8,128)(2,1)} fusion(bf16[64,128,512]{2,1,0:T(8,128)(2,1)} %bitcast.21, s32[1024]{0:T(1024)S(1)} %pad_clamp_fusion.1), kind=kCustom, calls=%fused_computation | custom fusion | bytes 16777472 | tf_op jit(solution)/shard_map/jit(_take)/gather | solution.py:21
  131.5 7.8 %bitcast_select_fusion = bf16[8192,512]{1,0:T(8,128)(2,1)} fusion(bf16[64,128,512]{2,1,0:T(8,128)(2,1)} %gather_fusion, pred[8192]{0:T(1024)(128)(4,1)S(1)} %broadcast_bitcast_fusion), kind=kLoop, calls=%fused_computation.3 | loop fusion | flops 4194304 | bytes 16785408 | tf_op jit(solution)/shard_map/jit(_take)/select_n | solution.py:21
  139.4 75.9 %all-gather.3.cloned.1.call-done = bf16[1024,8192]{1,0:T(8,128)(2,1)} async-done(((bf16[1024,512]{1,0:T(8,128)(2,1)}), bf16[1024,8192]{1,0:T(8,128)(2,1)}) %all-gather.3.cloned.1.call-update) | async-done | bytes 16777232 | tf_op jit(solution)/shard_map/all_gather | solution.py:25
  215.3 0.3 mul.39
  215.6 16.4 %select_reduce_fusion = (f32[]{:T(128)}, bf16[1024,512]{1,0:T(8,128)(2,1)}) fusion(s32[512]{0:T(512)S(1)} %iota_add_fusion, s32[1024]{0:T(1024)S(1)} %add_bitcast_fusion, f32[128,8,4,128]{3,2,1,0:T(4,128)S(1)} %bitcast.23, bf16[1024,8192]{1,0:T(8,128)(2,1)} %all-gather.3.cloned.1.call-done, bf16[8192,512]{1,0:T(8,128)(2,1)} %bitcast_select_fusion), kind=kOutput, calls=%fused_computation.6 | convolution fusion | flops 8592556032 | bytes 28317700 | tf_op jit(solution)/shard_map/dot_general | solution.py:24
  232.1 65.7 %psum.7 = f32[]{:T(128)} all-reduce(f32[]{:T(128)} %get-tuple-element.2), channel_id=1, replica_groups=mesh['row'=8,'col'=16] {'row','col'}, use_global_device_ids=true, to_apply=%region_2.3 | all-reduce | flops 1 | bytes 8 | tf_op jit(solution)/shard_map/psum | solution.py:39
  (8 shorter events, 0.0 us)
Async XLA Ops:
  7.2 115.5 %all-gather.5.cloned.1.call-start = ((), (), s32[]{:S(2)}) async-start(), calls=%async_computation.1 | async-start | bytes 9437184 | tf_op jit(solution)/shard_map/all_gather | solution.py:15
  10.7 204.6 %all-gather.3.cloned.1.call-start = ((), (), s32[]{:S(2)}) async-start(), calls=%async_computation | async-start | bytes 17825792 | tf_op jit(solution)/shard_map/all_gather | solution.py:25
Sparse Core Ops, SparseCore 0:
  10.9 111.6 all-gather.4
  124.9 90.3 all-gather.2
where the time goes:
time: 305 us
  waiting for transfers between devices  184 us (60%)
  blocking collectives  65.7 us (22%)
  matrix products  16.4 us (5%)
  between operations  14.1 us (5%)
  other arithmetic  12.3 us (4%)
  local copies, waits for them, and re-layouts  11.9 us (4%)
    all_gather x1, waiting for transfers between devices, on_device(): stacked = lax.all_gather(masked, 'row', axis=0, tiled=True)  107 us
    all_gather x1, waiting for transfers between devices, on_device(): lax.all_gather(masked, 'col', axis=1, tiled=True)  75.9 us
    psum x1, blocking collectives, on_device(): occupation = lax.psum(partial_trace, ('row', 'col'))  65.7 us
    dot_general x1, matrix products, on_device(): jnp.dot(lax.all_gather(masked, 'col', axis=1, tiled=True), natural, prefe...  16.4 us
    gather x1, local copies, waits for them, and re-layouts, on_device(): jnp.take(stacked.reshape(all_blocks, block_size, -1), inverse, axis=0)  8.9 us
    select_n x2, other arithmetic, on_device(): jnp.take(stacked.reshape(all_blocks, block_size, -1), inverse, axis=0)  7.84 us
  transfers between devices with their start and end apart: 2, of which 2 were waited for; matrix products, arithmetic and copies ran while one was open for 7% of the time, Pallas kernels for 0%

commit v1 on v0

v1 whole, which is shorter than its diff:
```python
import jax
import jax.numpy as jnp
from jax import lax
from jax.experimental import pallas as pl
from jax.experimental.pallas import tpu as pltpu
from jax.sharding import PartitionSpec as P

BS = 128
CAP = 6
LIST = 128
CHUNKS = 2
PART = BS // CHUNKS
COPIES = 96
IX_C1B, IX_C1O, IX_C2, IX_C3, IX_R1B, IX_R1O, IX_R2, IX_R3 = range(0, 64, 8)
IX_MATCH = 64
MESH = pl.DeviceIdType.MESH


class Path:
    def __init__(self, refs):
        refs = list(refs)
        take = lambda: [refs.pop(0) for _ in range(CHUNKS)]
        self.first, self.send, self.send2 = take(), take(), take()
        self.second, self.third = take(), take()
        (self.l_own, self.l_in1, self.l_send2, self.l_own2, self.l_in2,
         self.l_send3, self.l_in3, self.l_final) = refs


def kernel(values, pattern_in, filter_in, assignment_in, out, occupation, *refs):
    refs = list(refs)
    take = lambda count: [refs.pop(0) for _ in range(count)]
    own, pattern, other_pattern, filter_mask, assignment = take(5)
    other = take(CHUNKS)
    C, R = Path(take(5 * CHUNKS + 8)), Path(take(5 * CHUNKS + 8))
    columns_panel, = take(1)
    rows = take(8)
    tacc, trecv, finished, table, load_sem, out_sem, send_sem, recv_sem = take(8)

    row, col = lax.axis_index("row"), lax.axis_index("col")
    x, y_hi = row // 2, row % 2
    y_lo, z, core = col // 8, (col // 2) % 4, col % 2

    def partners(position):
        even, odd = position + 1 - 2 * (position % 2), 3 - position
        a = even * (1 - core) + odd * core
        b = odd * (1 - core) + even * core
        return a, b, (position + 2) % 4

    xa, xb, xd = partners(x)
    za, zb, zd = partners(z)
    dev_xa, dev_xb = (xa * 2 + y_hi, col), (xb * 2 + y_hi, col)
    dev_yh = (x * 2 + 1 - y_hi, col)
    dev_za = (row, y_lo * 8 + za * 2 + core)
    dev_zb = (row, y_lo * 8 + zb * 2 + core)
    dev_yl = (row, (1 - y_lo) * 8 + z * 2 + core)
    other_col = col + 1 - 2 * core
    dev_core = (row, other_col)

    remote = []

    def copy(src, dst, device):
        index = len(remote)
        remote.append(pltpu.make_async_remote_copy(
            src_ref=src, dst_ref=dst, send_sem=send_sem.at[index],
            recv_sem=recv_sem.at[index], device_id=device, device_id_type=MESH,
        ))
        return remote[-1]

    def start(*copies):
        for one in copies:
            one.start()

    def landed(*copies):
        for one in copies:
            one.wait_recv()

    small = [
        pltpu.make_async_copy(src, dst, load_sem.at[4 + i])
        for i, (src, dst) in enumerate(
            ((pattern_in, pattern), (assignment_in, assignment), (filter_in, filter_mask))
        )
    ]
    loads = [
        pltpu.make_async_copy(values.at[:, :, q * BS:(q + 1) * BS], own.at[q], load_sem.at[q])
        for q in range(4)
    ]
    start(*small, *loads)
    barrier = pltpu.get_barrier_semaphore()
    for device in (dev_xa, dev_xb, dev_yh, dev_za, dev_zb, dev_yl, dev_core):
        pl.semaphore_signal(barrier, inc=1, device_id=device, device_id_type=MESH)

    zero = jnp.zeros((PART, BS), jnp.bfloat16)
    for path in (C, R):
        for k in range(CHUNKS):
            path.first[k][4 * CAP] = zero
            path.second[k][2 * CAP] = zero
            path.third[k][2 * CAP] = zero
    for ref in rows:
        ref[CAP] = jnp.zeros((BS, BS), jnp.bfloat16)

    def part(k):
        return slice(k * PART, (k + 1) * PART)

    def rank(flags):
        count = jnp.int32(0)
        places = [jnp.int32(0)] * CAP
        for t, flag in enumerate(flags):
            for j in range(min(CAP, t + 1)):
                places[j] = jnp.where((flag != 0) & (count == j), t, places[j])
            count = count + flag
        return places, count

    def rank_column(role, q):
        places, count = rank([pattern[q, t] for t in range(8)])
        C.l_own[role * LIST] = count
        for j in range(CAP):
            name = assignment[row * 8 + places[j]]
            C.l_own[role * LIST + 1 + j] = jnp.where(j < count, name, -1)
        return q, places, count

    def pack_column(ranked, k, dst, first):
        q, places, count = ranked
        for j in range(CAP):
            block = own[q, places[j], part(k), :]
            dst[first + j] = jnp.where(j < count, block, zero)

    for one in small:
        one.wait()
    ranked_columns = [rank_column(role, q) for role, q in enumerate((x, xb, xa, xd))]
    for one in loads:
        one.wait()
    for k in range(CHUNKS):
        pack_column(ranked_columns[2], k, C.send[k], 0)
        pack_column(ranked_columns[3], k, C.send[k], CAP)

    half = (1 - core) * 4
    r0m = copy(pattern, other_pattern, dev_core)
    r0 = [copy(own.at[:, pl.ds(half, 4), part(k)], other[k], dev_core) for k in range(CHUNKS)]

    def first_copies(path, device):
        return (
            copy(path.l_own.at[pl.ds(2 * LIST, 2 * LIST)], path.l_in1, device),
            [copy(path.send[k], path.first[k].at[pl.ds(2 * CAP, 2 * CAP)], device) for k in range(CHUNKS)],
        )

    c1m, c1 = first_copies(C, dev_xa)
    r1m, r1 = first_copies(R, dev_za)

    pl.semaphore_wait(barrier, 7)
    start(r0m, c1m)
    for k in range(CHUNKS):
        start(r0[k], c1[k])
    for k in range(CHUNKS):
        pack_column(ranked_columns[0], k, C.first[k], 0)
        pack_column(ranked_columns[1], k, C.first[k], CAP)

    def rank_row(role, q):
        line = core * 4 + q
        places, count = rank(
            [pattern[t, line] for t in range(4)] + [other_pattern[t, line] for t in range(4)]
        )
        R.l_own[role * LIST] = count
        for j in range(CAP):
            name = jnp.where(places[j] < 4, col * 4, other_col * 4 - 4) + places[j]
            R.l_own[role * LIST + 1 + j] = jnp.where(j < count, name, -1)
        return line, q, places, count

    def pack_row(ranked, k, dst, first):
        line, q, places, count = ranked
        for j in range(CAP):
            mine = places[j] < 4
            place = jnp.where(mine, places[j], places[j] - 4)
            block = jnp.where(mine, own[place, line, part(k), :], other[k][place, q])
            dst[first + j] = jnp.where(j < count, block, zero)

    landed(r0m)
    ranked_rows = [rank_row(role, q) for role, q in enumerate((z, zb, za, zd))]
    start(r1m)
    for k in range(CHUNKS):
        landed(r0[k])
        pack_row(ranked_rows[2], k, R.send[k], 0)
        pack_row(ranked_rows[3], k, R.send[k], CAP)
        start(r1[k])

    def merge(l1, at1, l2, at2, lout, ix, base1, base2, zero_slot):
        n1, n2 = l1[at1], l2[at2]
        lout[0] = n1 + n2
        for j in range(CAP):
            rest = jnp.clip(j - n1, 0, CAP - 1)
            in1, in2 = j < n1, j - n1 < n2
            lout[1 + j] = jnp.where(in1, l1[at1 + 1 + j], jnp.where(in2, l2[at2 + 1 + rest], -1))
            table[ix + j] = jnp.where(in1, base1 + j, jnp.where(in2, base2 + rest, zero_slot))

    def move(src, ix, dst):
        for j in range(CAP):
            dst[j] = src[table[ix + j]]

    def six(ref, k, first=0):
        return ref[k].at[pl.ds(first, CAP)]

    def later_copies(path, device2, device3):
        return (
            copy(path.l_send2, path.l_in2, device2),
            [copy(path.send2[k], six(path.second, k, CAP), device2) for k in range(CHUNKS)],
            copy(path.l_send3, path.l_in3, device3),
            [copy(six(path.third, k), six(path.third, k, CAP), device3) for k in range(CHUNKS)],
        )

    c2m, c2, c3m, c3 = later_copies(C, dev_xb, dev_yh)
    r2m, r2, r3m, r3 = later_copies(R, dev_zb, dev_yl)

    def lists1(path, in_copy, out_copy, ix_b, ix_o):
        landed(in_copy)
        merge(path.l_own, LIST, path.l_in1, LIST, path.l_send2, ix_b, CAP, 3 * CAP, 4 * CAP)
        start(out_copy)
        merge(path.l_own, 0, path.l_in1, 0, path.l_own2, ix_o, 0, 2 * CAP, 4 * CAP)

    def lists2(path, in_copy, out_copy, ix):
        landed(in_copy)
        merge(path.l_own2, 0, path.l_in2, 0, path.l_send3, ix, 0, CAP, 2 * CAP)
        start(out_copy)

    def lists3(path, in_copy, out_copies, ix):
        landed(in_copy)
        merge(path.l_send3, 0, path.l_in3, 0, path.l_final, ix, 0, CAP, 2 * CAP)
        start(*out_copies)

    def blocks1(path, in_copies, out_copies, ix_b, ix_o, k):
        landed(in_copies[k])
        move(path.first[k], ix_b, path.send2[k])
        start(out_copies[k])
        move(path.first[k], ix_o, path.second[k])

    def blocks2(path, in_copies, out_copies, ix, k):
        landed(in_copies[k])
        move(path.second[k], ix, path.third[k])
        start(out_copies[k])

    def names(path, role):
        return path.l_final.at[pl.ds(role * LIST, LIST)]

    c4am, c4bm = copy(names(C, 0), names(C, 2), dev_xa), copy(names(C, 0), names(C, 1), dev_xb)
    c5m = copy(names(C, 1), names(C, 3), dev_xa)
    r4am, r4bm = copy(names(R, 0), names(R, 2), dev_za), copy(names(R, 0), names(R, 1), dev_zb)
    r5m = copy(names(R, 1), names(R, 3), dev_za)
    fm = [copy(names(R, role), names(R, 4 + role), dev_core) for role in range(4)]

    def column(role, k):
        return columns_panel.at[pl.ds(role * CAP, CAP), part(k)]

    def line_of(role, k):
        return rows[role].at[pl.ds(0, CAP), part(k)]

    each = range(CHUNKS)
    c4a = [copy(column(0, k), column(2, k), dev_xa) for k in each]
    c4b = [copy(column(0, k), column(1, k), dev_xb) for k in each]
    c5 = [copy(column(1, k), column(3, k), dev_xa) for k in each]
    r4a = [copy(line_of(0, k), line_of(2, k), dev_za) for k in each]
    r4b = [copy(line_of(0, k), line_of(1, k), dev_zb) for k in each]
    r5 = [copy(line_of(1, k), line_of(3, k), dev_za) for k in each]
    f = [[copy(line_of(role, k), line_of(4 + role, k), dev_core) for k in each] for role in range(4)]

    def blocks3_column(k):
        landed(c3[k])
        for j in range(CAP):
            columns_panel[j, part(k), :] = C.third[k][table[IX_C3 + j]]
        start(c4b[k], c4a[k])

    def blocks3_row(k):
        landed(r3[k])
        for j in range(CAP):
            rows[0][j, part(k), :] = R.third[k][table[IX_R3 + j]]
        start(r4b[k], r4a[k], f[0][k])

    def squares(ref):
        total = jnp.zeros((8, BS), jnp.float32)
        for i in range(2 * CAP):
            block = ref[i].astype(jnp.float32)
            total = total + jnp.sum((block * block).reshape(PART // 8, 8, BS), axis=0)
        return total

    trace_devices = (dev_core, dev_xa, dev_za, dev_xb, dev_zb, dev_yh, dev_yl)
    trace = [copy(tacc.at[i], trecv.at[i], trace_devices[i]) for i in range(7)]

    def trace_step(i):
        landed(trace[i])
        tacc[i + 1] = tacc[i] + trecv[i]
        if i < 6:
            start(trace[i + 1])

    for k in each:
        pack_row(ranked_rows[0], k, R.first[k], 0)
        pack_row(ranked_rows[1], k, R.first[k], CAP)
    total = jnp.zeros((8, BS), jnp.float32)
    for k in each:
        total = total + squares(C.send[k])
        total = total + squares(C.first[k])
    tacc[0] = total
    start(trace[0])

    row_lag = 0.75
    steps = []
    for k in each:
        steps += [
            (1 + k, lambda k=k: blocks1(C, c1, c2, IX_C1B, IX_C1O, k)),
            (2 + k, lambda k=k: blocks2(C, c2, c3, IX_C2, k)),
            (3 + k, lambda k=k: blocks3_column(k)),
            (4 + k, lambda k=k: (landed(c4b[k]), start(c5[k]))),
            (1 + k + row_lag, lambda k=k: blocks1(R, r1, r2, IX_R1B, IX_R1O, k)),
            (2 + k + row_lag, lambda k=k: blocks2(R, r2, r3, IX_R2, k)),
            (3 + k + row_lag, lambda k=k: blocks3_row(k)),
            (4 + k + row_lag, lambda k=k: (landed(r4b[k]), start(r5[k], f[1][k]))),
            (4.2 + k + row_lag, lambda k=k: (landed(r4a[k]), start(f[2][k]))),
            (5 + k + row_lag, lambda k=k: (landed(r5[k]), start(f[3][k]))),
        ]
    steps += [
        (0.9, lambda: lists1(C, c1m, c2m, IX_C1B, IX_C1O)),
        (1.7, lambda: lists1(R, r1m, r2m, IX_R1B, IX_R1O)),
        (1.8, lambda: trace_step(0)),
        (1.9, lambda: lists2(C, c2m, c3m, IX_C2)),
        (2.7, lambda: lists2(R, r2m, r3m, IX_R2)),
        (2.9, lambda: lists3(C, c3m, (c4bm, c4am), IX_C3)),
        (3.1, lambda: trace_step(1)),
        (3.7, lambda: lists3(R, r3m, (r4bm, r4am, fm[0]), IX_R3)),
        (3.8, lambda: trace_step(2)),
        (4.1, lambda: (landed(c4bm), start(c5m))),
        (4.3, lambda: trace_step(3)),
        (4.8, lambda: (landed(r4bm), start(r5m, fm[1]))),
        (5.01, lambda: (landed(r4am), start(fm[2]))),
        (5.1, lambda: trace_step(4)),
        (5.8, lambda: (landed(r5m), start(fm[3]))),
        (5.85, lambda: trace_step(5)),
    ]
    for _, step in sorted(steps, key=lambda one: one[0]):
        step()

    late = [*r5, *f[1], *f[2], *f[3], r5m, *fm, *c5, c5m, *trace[5:]]
    for one in remote:
        if not any(one is other_one for other_one in late):
            one.wait_send()

    landed(c4am, c5m, *fm)

    def match(row_role, carry):
        have = [R.l_final[row_role * LIST + 1 + i] for i in range(CAP)]
        for t in range(4 * CAP):
            wanted = C.l_final[(t // CAP) * LIST + 1 + t % CAP]
            slot = jnp.int32(CAP)
            for i in range(CAP):
                slot = jnp.where(have[i] == wanted, i, slot)
            table[IX_MATCH + row_role * 4 * CAP + t] = slot
        return carry

    lax.fori_loop(0, 8, match, 0)
    trace_step(6)
    occupation[0, 0] = jnp.sum(tacc[7])

    for k in each:
        landed(c4a[k], c5[k])

    column_of = (x, xb, xa, xd)
    line_by_role = (
        [core * 4 + position for position in (z, zb, za, zd)]
        + [(1 - core) * 4 + position for position in (z, za, zb, zd)]
    )

    leaving = [
        pltpu.make_async_copy(finished.at[role], out.at[line_by_role[role]], out_sem.at[role])
        for role in range(8)
    ]

    def product(row_roles):
        for c in range(4):
            left = []
            for role in row_roles:
                base = IX_MATCH + (role * 4 + c) * CAP
                left.append(jnp.concatenate([rows[role][table[base + j]] for j in range(CAP)], axis=1))
            right = columns_panel[c * CAP:(c + 1) * CAP].reshape(CAP * BS, BS)
            total = jnp.dot(
                jnp.concatenate(left, axis=0), right, preferred_element_type=jnp.float32
            )
            q = column_of[c]
            for i, role in enumerate(row_roles):
                line = line_by_role[role]
                kept = jnp.where(filter_mask[q, line] != 0, total[i * BS:(i + 1) * BS], 0.0)
                finished[role, :, pl.ds(pl.multiple_of(q * BS, BS), BS)] = kept.astype(jnp.bfloat16)
        start(*[leaving[role] for role in row_roles])

    product((0, 1))
    product((2, 3))
    for role in (0, 1):
        landed(*f[role])
    product((4, 5))
    for role in (2, 3):
        landed(*f[role])
    product((6, 7))

    for one in late:
        one.wait_send()
    for one in leaving:
        one.wait()


def on_device(values, pattern, filter_mask, assignment):
    hbm = pl.BlockSpec(memory_space=pltpu.HBM)
    parts = lambda count: [pltpu.VMEM((count, PART, BS), jnp.bfloat16)] * CHUNKS
    lists = lambda *counts: [pltpu.SMEM((count * LIST,), jnp.int32) for count in counts]

    def path(final):
        return [
            *parts(4 * CAP + 1), *parts(2 * CAP), *parts(CAP), *parts(2 * CAP + 1),
            *parts(2 * CAP + 1), *lists(4, 2, 1, 1, 1, 1, 1, final),
        ]

    product, occupation = pl.pallas_call(
        kernel,
        out_shape=(
            jax.ShapeDtypeStruct((8, BS, 4 * BS), jnp.bfloat16),
            jax.ShapeDtypeStruct((1, 1), jnp.float32),
        ),
        in_specs=[hbm] * 4,
        out_specs=(hbm, pl.BlockSpec(memory_space=pltpu.SMEM)),
        scratch_shapes=[
            pltpu.VMEM((4, 8, BS, BS), jnp.bfloat16),
            pltpu.SMEM((4, 8), jnp.int32),
            pltpu.SMEM((4, 8), jnp.int32),
            pltpu.SMEM((4, 8), jnp.int32),
            pltpu.SMEM((64,), jnp.int32),
            *[pltpu.VMEM((4, 4, PART, BS), jnp.bfloat16)] * CHUNKS,
            *path(4),
            *path(8),
            pltpu.VMEM((4 * CAP, BS, BS), jnp.bfloat16),
            *[pltpu.VMEM((CAP + 1, BS, BS), jnp.bfloat16)] * 8,
            pltpu.VMEM((8, 8, BS), jnp.float32),
            pltpu.VMEM((7, 8, BS), jnp.float32),
            pltpu.VMEM((8, BS, 4 * BS), jnp.bfloat16),
            pltpu.SMEM((IX_MATCH + 8 * 4 * CAP,), jnp.int32),
            pltpu.SemaphoreType.DMA((7,)),
            pltpu.SemaphoreType.DMA((8,)),
            pltpu.SemaphoreType.DMA((COPIES,)),
            pltpu.SemaphoreType.DMA((COPIES,)),
        ],
        compiler_params=pltpu.CompilerParams(
            collective_id=0, has_side_effects=True, vmem_limit_bytes=63 * 1024 * 1024
        ),
        cost_estimate=pl.CostEstimate(
            flops=2 * 192 * BS**3, bytes_accessed=4 * 1024 * 1024, transcendentals=0
        ),
    )(values.reshape(8, BS, 4 * BS), pattern.T, filter_mask.T, assignment)
    return product.reshape(values.shape), occupation[0, 0]


def solution(mesh):
    in_specs = (P("row", "col"), P("row", "col"), P("row", "col"), P())
    out_specs = (P("row", "col"), P())
    return jax.shard_map(
        on_device, mesh=mesh, in_specs=in_specs, out_specs=out_specs, check_vma=False
    )
```

time: 305 us -> 44.8 us (0.15)
  waiting for transfers between devices: 184 us -> 0 us
  blocking collectives: 65.7 us -> 0 us
  Pallas kernels: 0 us -> 39.4 us
  matrix products: 16.4 us -> 0 us
  other arithmetic: 12.3 us -> 0 us
  between operations: 14.1 us -> 2.33 us
  local copies, waits for them, and re-layouts: 11.9 us -> 2.26 us
    all_gather x2 -> x0, waiting for transfers between devices: 183 us -> none  [the longest x1 107 us: on_device(): stacked = lax.all_gather(masked, 'row', axis=0, tiled=True)]
    psum x1 -> x0, blocking collectives: 65.7 us -> none  [on_device(): occupation = lax.psum(partial_trace, ('row', 'col'))]
    pallas_call x0 -> x1, Pallas kernels: none -> 39.4 us  [on_device(): pl.pallas_call(kernel, out_shape=(jax.ShapeDtypeStruct((8, BS, 4 * BS), j...]
    dot_general x1 -> x0, matrix products: 16.4 us -> none  [on_device(): jnp.dot(lax.all_gather(masked, 'col', axis=1, tiled=True), natural, prefe...]
    gather x2 -> x0, local copies, waits for them, and re-layouts: 10.2 us -> none  [the longest x1 8.9 us: on_device(): jnp.take(stacked.reshape(all_blocks, block_size, -1), inverse, axis=0)]
    select_n x4 -> x0, other arithmetic: 8.51 us -> none  [the longest x2 7.84 us: on_device(): jnp.take(stacked.reshape(all_blocks, block_size, -1), inverse, axis=0)]
  transfers between devices with their start and end apart: 2 -> 0, of which waited for: 2 -> 0; matrix products, arithmetic and copies ran while one was open for 7% -> 0% of each run, Pallas kernels for 0% -> 0%
where the time goes in v1:
time: 44.8 us; the launch traced here: 44 us
  Pallas kernels  39.4 us (88%)
  between operations  2.33 us (5%)
  local copies, waits for them, and re-layouts  2.26 us (5%)
    pallas_call x1, Pallas kernels, on_device(): pl.pallas_call(kernel, out_shape=(jax.ShapeDtypeStruct((8, BS, 4 * BS), j...  39.4 us
    unnamed x1, local copies, waits for them, and re-layouts  2.26 us

profile of v1, /device:TPU:1, one launch (start us, length us, event | category | flops | bytes accessed | tf_op | source)
XLA Modules:
  0.0 44.0 jit_solution(15204000778339388354)
XLA Ops:
  0.6 39.4 %shard_map.59 = (bf16[8,128,512]{2,1,0:T(8,128)(2,1)}, f32[1,1]{1,0:T(1,128)}) custom-call(bf16[8,128,512]{2,1,0:T(8,128)(2,1)} %bitcast.6, s32[4,8]{1,0:T(4,128)} %bitcast.7, s32[4,8]{1,0:T(4,128)} %bitcast.8, s32[64]{0:T(128)} %assignment_in.1), custom_call_target="tpu_custom_call" | custom-call | flops 805306368 | bytes 4194304 | tf_op jit(solution)/shard_map/pallas_call | solution.py:415
  40.1 2.3 %copy.8 = bf16[1024,512]{1,0:T(8,128)(2,1)} copy(bf16[1024,512]{1,0:T(8,128)(2,1)} %bitcast.5) | data formatting | bytes 2097152

commit v2 on v1

--- a/solution.py
+++ b/solution.py
@@ -8,9 +8,9 @@
 BS = 128
 CAP = 6
 LIST = 128
-CHUNKS = 2
+CHUNKS = 4
 PART = BS // CHUNKS
-COPIES = 96
+COPIES = 160
 IX_C1B, IX_C1O, IX_C2, IX_C3, IX_R1B, IX_R1O, IX_R2, IX_R3 = range(0, 64, 8)
 IX_MATCH = 64
 MESH = pl.DeviceIdType.MESH
@@ -298,38 +298,40 @@
     tacc[0] = total
     start(trace[0])
 
-    row_lag = 0.75
+    row_lag, gap = 0.7, 1.7 / CHUNKS
     steps = []
     for k in each:
+        at = 1 + k * gap
         steps += [
-            (1 + k, lambda k=k: blocks1(C, c1, c2, IX_C1B, IX_C1O, k)),
-            (2 + k, lambda k=k: blocks2(C, c2, c3, IX_C2, k)),
-            (3 + k, lambda k=k: blocks3_column(k)),
-            (4 + k, lambda k=k: (landed(c4b[k]), start(c5[k]))),
-            (1 + k + row_lag, lambda k=k: blocks1(R, r1, r2, IX_R1B, IX_R1O, k)),
-            (2 + k + row_lag, lambda k=k: blocks2(R, r2, r3, IX_R2, k)),
-            (3 + k + row_lag, lambda k=k: blocks3_row(k)),
-            (4 + k + row_lag, lambda k=k: (landed(r4b[k]), start(r5[k], f[1][k]))),
-            (4.2 + k + row_lag, lambda k=k: (landed(r4a[k]), start(f[2][k]))),
-            (5 + k + row_lag, lambda k=k: (landed(r5[k]), start(f[3][k]))),
+            (at, lambda k=k: blocks1(C, c1, c2, IX_C1B, IX_C1O, k)),
+            (at + 1, lambda k=k: blocks2(C, c2, c3, IX_C2, k)),
+            (at + 2, lambda k=k: blocks3_column(k)),
+            (at + 3, lambda k=k: (landed(c4b[k]), start(c5[k]))),
+            (at + row_lag, lambda k=k: blocks1(R, r1, r2, IX_R1B, IX_R1O, k)),
+            (at + 1 + row_lag, lambda k=k: blocks2(R, r2, r3, IX_R2, k)),
+            (at + 2 + row_lag, lambda k=k: blocks3_row(k)),
+            (at + 3 + row_lag, lambda k=k: (landed(r4b[k]), start(r5[k], f[1][k]))),
+            (at + 3.2 + row_lag, lambda k=k: (landed(r4a[k]), start(f[2][k]))),
+            (at + 4 + row_lag, lambda k=k: (landed(r5[k]), start(f[3][k]))),
         ]
+    last = (CHUNKS - 1) * gap + 0.02
     steps += [
-        (0.9, lambda: lists1(C, c1m, c2m, IX_C1B, IX_C1O)),
-        (1.7, lambda: lists1(R, r1m, r2m, IX_R1B, IX_R1O)),
-        (1.8, lambda: trace_step(0)),
-        (1.9, lambda: lists2(C, c2m, c3m, IX_C2)),
-        (2.7, lambda: lists2(R, r2m, r3m, IX_R2)),
-        (2.9, lambda: lists3(C, c3m, (c4bm, c4am), IX_C3)),
-        (3.1, lambda: trace_step(1)),
-        (3.7, lambda: lists3(R, r3m, (r4bm, r4am, fm[0]), IX_R3)),
-        (3.8, lambda: trace_step(2)),
-        (4.1, lambda: (landed(c4bm), start(c5m))),
-        (4.3, lambda: trace_step(3)),
-        (4.8, lambda: (landed(r4bm), start(r5m, fm[1]))),
-        (5.01, lambda: (landed(r4am), start(fm[2]))),
-        (5.1, lambda: trace_step(4)),
-        (5.8, lambda: (landed(r5m), start(fm[3]))),
-        (5.85, lambda: trace_step(5)),
+        (0.99, lambda: lists1(C, c1m, c2m, IX_C1B, IX_C1O)),
+        (0.99 + row_lag, lambda: lists1(R, r1m, r2m, IX_R1B, IX_R1O)),
+        (1.01 + row_lag, lambda: trace_step(0)),
+        (1.99, lambda: lists2(C, c2m, c3m, IX_C2)),
+        (1.99 + row_lag, lambda: lists2(R, r2m, r3m, IX_R2)),
+        (2.99, lambda: lists3(C, c3m, (c4bm, c4am), IX_C3)),
+        (2 + last, lambda: trace_step(1)),
+        (2.99 + row_lag, lambda: lists3(R, r3m, (r4bm, r4am, fm[0]), IX_R3)),
+        (2 + last + row_lag, lambda: trace_step(2)),
+        (4.01, lambda: (landed(c4bm), start(c5m))),
+        (3 + last, lambda: trace_step(3)),
+        (4.01 + row_lag, lambda: (landed(r4bm), start(r5m, fm[1]))),
+        (4.21 + row_lag, lambda: (landed(r4am), start(fm[2]))),
+        (3 + last + row_lag, lambda: trace_step(4)),
+        (5.01 + row_lag, lambda: (landed(r5m), start(fm[3]))),
+        (4 + last + row_lag, lambda: trace_step(5)),
     ]
     for _, step in sorted(steps, key=lambda one: one[0]):
         step()

time: 44.8 us -> 45.1 us (level)
  no operation moved by 1% of the time
where the time goes in v2:
time: 45.1 us; the launch traced here: 44.3 us
  Pallas kernels  39.7 us (88%)
  between operations  2.33 us (5%)
  local copies, waits for them, and re-layouts  2.26 us (5%)
    pallas_call x1, Pallas kernels, on_device(): pl.pallas_call(kernel, out_shape=(jax.ShapeDtypeStruct((8, BS, 4 * BS), j...  39.7 us
    unnamed x1, local copies, waits for them, and re-layouts  2.26 us

profile of v2, /device:TPU:1, one launch (start us, length us, event | category | flops | bytes accessed | tf_op | source)
XLA Modules:
  0.0 44.3 jit_solution(8260930857717322223)
XLA Ops:
  0.6 39.7 %shard_map.59 = (bf16[8,128,512]{2,1,0:T(8,128)(2,1)}, f32[1,1]{1,0:T(1,128)}) custom-call(bf16[8,128,512]{2,1,0:T(8,128)(2,1)} %bitcast.6, s32[4,8]{1,0:T(4,128)} %bitcast.7, s32[4,8]{1,0:T(4,128)} %bitcast.8, s32[64]{0:T(128)} %assignment_in.1), custom_call_target="tpu_custom_call" | custom-call | flops 805306368 | bytes 4194304 | tf_op jit(solution)/shard_map/pallas_call | solution.py:417
  40.3 2.3 %copy.8 = bf16[1024,512]{1,0:T(8,128)(2,1)} copy(bf16[1024,512]{1,0:T(8,128)(2,1)} %bitcast.5) | data formatting | bytes 2097152

commit v3 on v1

--- a/solution.py
+++ b/solution.py
@@ -243,7 +243,7 @@
     c5m = copy(names(C, 1), names(C, 3), dev_xa)
     r4am, r4bm = copy(names(R, 0), names(R, 2), dev_za), copy(names(R, 0), names(R, 1), dev_zb)
     r5m = copy(names(R, 1), names(R, 3), dev_za)
-    fm = [copy(names(R, role), names(R, 4 + role), dev_core) for role in range(4)]
+    fm = copy(R.l_final.at[pl.ds(0, 4 * LIST)], R.l_final.at[pl.ds(4 * LIST, 4 * LIST)], dev_core)
 
     def column(role, k):
         return columns_panel.at[pl.ds(role * CAP, CAP), part(k)]
@@ -297,6 +297,19 @@
         total = total + squares(C.first[k])
     tacc[0] = total
     start(trace[0])
+
+    def match(row_role, carry):
+        have = [R.l_final[row_role * LIST + 1 + i] for i in range(CAP)]
+        for t in range(4 * CAP):
+            wanted = C.l_final[(t // CAP) * LIST + 1 + t % CAP]
+            slot = jnp.int32(CAP)
+            for i in range(CAP):
+                slot = jnp.where(have[i] == wanted, i, slot)
+            table[IX_MATCH + row_role * 4 * CAP + t] = slot
+        return carry
+
+    def match_rows(first_role):
+        lax.fori_loop(first_role, first_role + 4, match, 0)
 
     row_lag = 0.75
     steps = []
@@ -315,45 +328,25 @@
         ]
     steps += [
         (0.9, lambda: lists1(C, c1m, c2m, IX_C1B, IX_C1O)),
-        (1.7, lambda: lists1(R, r1m, r2m, IX_R1B, IX_R1O)),
+        (1.1, lambda: lists1(R, r1m, r2m, IX_R1B, IX_R1O)),
+        (1.3, lambda: lists2(C, c2m, c3m, IX_C2)),
         (1.8, lambda: trace_step(0)),
-        (1.9, lambda: lists2(C, c2m, c3m, IX_C2)),
-        (2.7, lambda: lists2(R, r2m, r3m, IX_R2)),
-        (2.9, lambda: lists3(C, c3m, (c4bm, c4am), IX_C3)),
+        (2.1, lambda: lists2(R, r2m, r3m, IX_R2)),
+        (2.2, lambda: lists3(C, c3m, (c4bm, c4am), IX_C3)),
+        (2.9, lambda: lists3(R, r3m, (r4bm, r4am), IX_R3)),
         (3.1, lambda: trace_step(1)),
-        (3.7, lambda: lists3(R, r3m, (r4bm, r4am, fm[0]), IX_R3)),
-        (3.8, lambda: trace_step(2)),
-        (4.1, lambda: (landed(c4bm), start(c5m))),
+        (3.2, lambda: (landed(c4bm), start(c5m))),
+        (3.8, lambda: (landed(r4bm), start(r5m))),
+        (3.85, lambda: trace_step(2)),
+        (4.05, lambda: (landed(r4am, r5m), start(fm))),
+        (4.1, lambda: (landed(c4am, c5m), match_rows(0))),
         (4.3, lambda: trace_step(3)),
-        (4.8, lambda: (landed(r4bm), start(r5m, fm[1]))),
-        (5.01, lambda: (landed(r4am), start(fm[2]))),
+        (5.05, lambda: (landed(fm), match_rows(4))),
         (5.1, lambda: trace_step(4)),
-        (5.8, lambda: (landed(r5m), start(fm[3]))),
         (5.85, lambda: trace_step(5)),
     ]
     for _, step in sorted(steps, key=lambda one: one[0]):
         step()
-
-    late = [*r5, *f[1], *f[2], *f[3], r5m, *fm, *c5, c5m, *trace[5:]]
-    for one in remote:
-        if not any(one is other_one for other_one in late):
-            one.wait_send()
-
-    landed(c4am, c5m, *fm)
-
-    def match(row_role, carry):
-        have = [R.l_final[row_role * LIST + 1 + i] for i in range(CAP)]
-        for t in range(4 * CAP):
-            wanted = C.l_final[(t // CAP) * LIST + 1 + t % CAP]
-            slot = jnp.int32(CAP)
-            for i in range(CAP):
-                slot = jnp.where(have[i] == wanted, i, slot)
-            table[IX_MATCH + row_role * 4 * CAP + t] = slot
-        return carry
-
-    lax.fori_loop(0, 8, match, 0)
-    trace_step(6)
-    occupation[0, 0] = jnp.sum(tacc[7])
 
     for k in each:
         landed(c4a[k], c5[k])
@@ -395,7 +388,9 @@
         landed(*f[role])
     product((6, 7))
 
-    for one in late:
+    trace_step(6)
+    occupation[0, 0] = jnp.sum(tacc[7])
+    for one in remote:
         one.wait_send()
     for one in leaving:
         one.wait()

time: 44.8 us -> 44.6 us (level); the launches traced: 44 us -> 44.4 us
  no operation moved by 1% of the time
where the time goes in v3:
time: 44.6 us; the launch traced here: 44.4 us
  Pallas kernels  39.8 us (89%)
  between operations  2.33 us (5%)
  local copies, waits for them, and re-layouts  2.26 us (5%)
    pallas_call x1, Pallas kernels, on_device(): pl.pallas_call(kernel, out_shape=(jax.ShapeDtypeStruct((8, BS, 4 * BS), j...  39.8 us
    unnamed x1, local copies, waits for them, and re-layouts  2.26 us

profile of v3, /device:TPU:1, one launch (start us, length us, event | category | flops | bytes accessed | tf_op | source)
XLA Modules:
  0.0 44.4 jit_solution(3511561424549398812)
XLA Ops:
  0.6 39.8 %shard_map.59 = (bf16[8,128,512]{2,1,0:T(8,128)(2,1)}, f32[1,1]{1,0:T(1,128)}) custom-call(bf16[8,128,512]{2,1,0:T(8,128)(2,1)} %bitcast.6, s32[4,8]{1,0:T(4,128)} %bitcast.7, s32[4,8]{1,0:T(4,128)} %bitcast.8, s32[64]{0:T(128)} %assignment_in.1), custom_call_target="tpu_custom_call" | custom-call | flops 805306368 | bytes 4194304 | tf_op jit(solution)/shard_map/pallas_call | solution.py:410
  40.4 2.3 %copy.8 = bf16[1024,512]{1,0:T(8,128)(2,1)} copy(bf16[1024,512]{1,0:T(8,128)(2,1)} %bitcast.5) | data formatting | bytes 2097152

commit v4 on v3

--- a/solution.py
+++ b/solution.py
@@ -34,7 +34,7 @@
     C, R = Path(take(5 * CHUNKS + 8)), Path(take(5 * CHUNKS + 8))
     columns_panel, = take(1)
     rows = take(8)
-    tacc, trecv, finished, table, load_sem, out_sem, send_sem, recv_sem = take(8)
+    tacc, trecv, table, load_sem, send_sem, recv_sem = take(6)
 
     row, col = lax.axis_index("row"), lax.axis_index("col")
     x, y_hi = row // 2, row % 2
@@ -357,11 +357,6 @@
         + [(1 - core) * 4 + position for position in (z, za, zb, zd)]
     )
 
-    leaving = [
-        pltpu.make_async_copy(finished.at[role], out.at[line_by_role[role]], out_sem.at[role])
-        for role in range(8)
-    ]
-
     def product(row_roles):
         for c in range(4):
             left = []
@@ -376,8 +371,7 @@
             for i, role in enumerate(row_roles):
                 line = line_by_role[role]
                 kept = jnp.where(filter_mask[q, line] != 0, total[i * BS:(i + 1) * BS], 0.0)
-                finished[role, :, pl.ds(pl.multiple_of(q * BS, BS), BS)] = kept.astype(jnp.bfloat16)
-        start(*[leaving[role] for role in row_roles])
+                out[line, :, pl.ds(pl.multiple_of(q * BS, BS), BS)] = kept.astype(jnp.bfloat16)
 
     product((0, 1))
     product((2, 3))
@@ -392,8 +386,6 @@
     occupation[0, 0] = jnp.sum(tacc[7])
     for one in remote:
         one.wait_send()
-    for one in leaving:
-        one.wait()
 
 
 def on_device(values, pattern, filter_mask, assignment):
@@ -414,7 +406,7 @@
             jax.ShapeDtypeStruct((1, 1), jnp.float32),
         ),
         in_specs=[hbm] * 4,
-        out_specs=(hbm, pl.BlockSpec(memory_space=pltpu.SMEM)),
+        out_specs=(pl.BlockSpec(memory_space=pltpu.VMEM), pl.BlockSpec(memory_space=pltpu.SMEM)),
         scratch_shapes=[
             pltpu.VMEM((4, 8, BS, BS), jnp.bfloat16),
             pltpu.SMEM((4, 8), jnp.int32),
@@ -428,15 +420,13 @@
             *[pltpu.VMEM((CAP + 1, BS, BS), jnp.bfloat16)] * 8,
             pltpu.VMEM((8, 8, BS), jnp.float32),
             pltpu.VMEM((7, 8, BS), jnp.float32),
-            pltpu.VMEM((8, BS, 4 * BS), jnp.bfloat16),
             pltpu.SMEM((IX_MATCH + 8 * 4 * CAP,), jnp.int32),
             pltpu.SemaphoreType.DMA((7,)),
-            pltpu.SemaphoreType.DMA((8,)),
             pltpu.SemaphoreType.DMA((COPIES,)),
             pltpu.SemaphoreType.DMA((COPIES,)),
         ],
         compiler_params=pltpu.CompilerParams(
-            collective_id=0, has_side_effects=True, vmem_limit_bytes=63 * 1024 * 1024
+            collective_id=0, has_side_effects=True, vmem_limit_bytes=52 * 1024 * 1024
         ),
         cost_estimate=pl.CostEstimate(
             flops=2 * 192 * BS**3, bytes_accessed=4 * 1024 * 1024, transcendentals=0

time: 44.6 us -> 43.4 us (0.973)
  local copies, waits for them, and re-layouts: 2.26 us -> 1.65 us
  Pallas kernels: 39.8 us -> 39.2 us
    unnamed x1 -> x7, local copies, waits for them, and re-layouts: 2.26 us -> 1.65 us
    pallas_call x1, Pallas kernels: 39.8 us -> 39.2 us  [on_device(): pl.pallas_call(kernel, out_shape=(jax.ShapeDtypeStruct((8, BS, 4 * BS), j...]
where the time goes in v4:
time: 43.4 us; the launch traced here: 43.2 us
  Pallas kernels  39.2 us (90%)
  between operations  2.4 us (6%)
  local copies, waits for them, and re-layouts  1.65 us (4%)
    pallas_call x1, Pallas kernels, on_device(): pl.pallas_call(kernel, out_shape=(jax.ShapeDtypeStruct((8, BS, 4 * BS), j...  39.2 us
    unnamed x7, local copies, waits for them, and re-layouts  1.65 us

profile of v4, /device:TPU:1, one launch (start us, length us, event | category | flops | bytes accessed | tf_op | source)
XLA Modules:
  0.0 43.2 jit_solution(10117847145229902418)
XLA Ops:
  0.6 0.0 copy-start.1
  0.6 0.0 copy-start
  0.6 0.0 copy-start.2
  0.7 0.7 %copy-done.1 = s32[8,4]{0,1:T(4,128)S(1)} copy-done((s32[8,4]{0,1:T(4,128)S(1)}, s32[8,4]{0,1:T(4,128)}, u32[]{:S(2)}) %copy-start.1) | copy-done | bytes 152
  1.3 0.0 copy-done
  1.3 0.0 copy-done.2
  1.3 39.2 %shard_map.59 = (bf16[8,128,512]{2,1,0:T(8,128)(2,1)S(1)}, f32[1,1]{1,0:T(1,128)}) custom-call(bf16[8,128,512]{2,1,0:T(8,128)(2,1)} %bitcast.8, s32[4,8]{1,0:T(4,128)S(1)} %bitcast.6, s32[4,8]{1,0:T(4,128)S(1)} %bitcast.7, s32[64]{0:T(128)S(1)} %copy-done.2), custom_call_target="tpu_custom_call" | custom-call | flops 805306368 | bytes 4194304 | tf_op jit(solution)/shard_map/pallas_call | solution.py:402
  40.5 1.0 %copy.8 = bf16[1024,512]{1,0:T(8,128)(2,1)} copy(bf16[1024,512]{1,0:T(8,128)(2,1)S(1)} %bitcast.5) | data formatting | bytes 2097152
Async XLA Ops:
  0.6 0.7 %copy-start.1 = (s32[8,4]{0,1:T(4,128)S(1)}, s32[8,4]{0,1:T(4,128)}, u32[]{:S(2)}) copy-start(s32[8,4]{0,1:T(4,128)} %param.6) | copy-start | bytes 388
  0.6 0.7 %copy-start = (s32[8,4]{0,1:T(4,128)S(1)}, s32[8,4]{0,1:T(4,128)}, u32[]{:S(2)}) copy-start(s32[8,4]{0,1:T(4,128)} %param.5) | copy-start | bytes 388
  0.6 0.7 %copy-start.2 = (s32[64]{0:T(128)S(1)}, s32[64]{0:T(128)}, u32[]{:S(2)}) copy-start(s32[64]{0:T(128)} %assignment_in.1) | copy-start | bytes 772

commit v5 on v4

--- a/solution.py
+++ b/solution.py
@@ -310,6 +310,13 @@
 
     def match_rows(first_role):
         lax.fori_loop(first_role, first_role + 4, match, 0)
+
+    done = []
+
+    def sent(*copies):
+        for one in copies:
+            one.wait_send()
+            done.append(one)
 
     row_lag = 0.75
     steps = []
@@ -343,6 +350,7 @@
         (4.3, lambda: trace_step(3)),
         (5.05, lambda: (landed(fm), match_rows(4))),
         (5.1, lambda: trace_step(4)),
+        (5.5, lambda: sent(c1m, *c1, r0m, *r0, r1m, *r1, c2m, *c2, r2m, *r2)),
         (5.85, lambda: trace_step(5)),
     ]
     for _, step in sorted(steps, key=lambda one: one[0]):
@@ -378,6 +386,7 @@
     for role in (0, 1):
         landed(*f[role])
     product((4, 5))
+    sent(c3m, *c3, r3m, *r3, c4am, c4bm, r4am, r4bm, c5m, r5m, fm, *c4b, *trace[:5])
     for role in (2, 3):
         landed(*f[role])
     product((6, 7))
@@ -385,7 +394,8 @@
     trace_step(6)
     occupation[0, 0] = jnp.sum(tacc[7])
     for one in remote:
-        one.wait_send()
+        if not any(one is other_one for other_one in done):
+            one.wait_send()
 
 
 def on_device(values, pattern, filter_mask, assignment):

time: 43.4 us -> 43.2 us (level)
  no operation moved by 1% of the time
where the time goes in v5:
time: 43.2 us; the launch traced here: 43 us
  Pallas kernels  39 us (90%)
  between operations  2.4 us (6%)
  local copies, waits for them, and re-layouts  1.65 us (4%)
    pallas_call x1, Pallas kernels, on_device(): pl.pallas_call(kernel, out_shape=(jax.ShapeDtypeStruct((8, BS, 4 * BS), j...  39 us
    unnamed x7, local copies, waits for them, and re-layouts  1.65 us

profile of v5, /device:TPU:1, one launch (start us, length us, event | category | flops | bytes accessed | tf_op | source)
XLA Modules:
  0.0 43.0 jit_solution(5096027770779822006)
XLA Ops:
  0.6 0.0 copy-start.1
  0.6 0.0 copy-start
  0.6 0.0 copy-start.2
  0.7 0.7 %copy-done.1 = s32[8,4]{0,1:T(4,128)S(1)} copy-done((s32[8,4]{0,1:T(4,128)S(1)}, s32[8,4]{0,1:T(4,128)}, u32[]{:S(2)}) %copy-start.1) | copy-done | bytes 152
  1.3 0.0 copy-done
  1.3 0.0 copy-done.2
  1.3 39.0 %shard_map.59 = (bf16[8,128,512]{2,1,0:T(8,128)(2,1)S(1)}, f32[1,1]{1,0:T(1,128)}) custom-call(bf16[8,128,512]{2,1,0:T(8,128)(2,1)} %bitcast.8, s32[4,8]{1,0:T(4,128)S(1)} %bitcast.6, s32[4,8]{1,0:T(4,128)S(1)} %bitcast.7, s32[64]{0:T(128)S(1)} %copy-done.2), custom_call_target="tpu_custom_call" | custom-call | flops 805306368 | bytes 4194304 | tf_op jit(solution)/shard_map/pallas_call | solution.py:412
  40.3 1.0 %copy.8 = bf16[1024,512]{1,0:T(8,128)(2,1)} copy(bf16[1024,512]{1,0:T(8,128)(2,1)S(1)} %bitcast.5) | data formatting | bytes 2097152
Async XLA Ops:
  0.6 0.7 %copy-start.1 = (s32[8,4]{0,1:T(4,128)S(1)}, s32[8,4]{0,1:T(4,128)}, u32[]{:S(2)}) copy-start(s32[8,4]{0,1:T(4,128)} %param.6) | copy-start | bytes 388
  0.6 0.7 %copy-start = (s32[8,4]{0,1:T(4,128)S(1)}, s32[8,4]{0,1:T(4,128)}, u32[]{:S(2)}) copy-start(s32[8,4]{0,1:T(4,128)} %param.5) | copy-start | bytes 388
  0.6 0.7 %copy-start.2 = (s32[64]{0:T(128)S(1)}, s32[64]{0:T(128)}, u32[]{:S(2)}) copy-start(s32[64]{0:T(128)} %assignment_in.1) | copy-start | bytes 772

commit v6 on v5

--- a/solution.py
+++ b/solution.py
@@ -129,10 +129,6 @@
     ranked_columns = [rank_column(role, q) for role, q in enumerate((x, xb, xa, xd))]
     for one in loads:
         one.wait()
-    for k in range(CHUNKS):
-        pack_column(ranked_columns[2], k, C.send[k], 0)
-        pack_column(ranked_columns[3], k, C.send[k], CAP)
-
     half = (1 - core) * 4
     r0m = copy(pattern, other_pattern, dev_core)
     r0 = [copy(own.at[:, pl.ds(half, 4), part(k)], other[k], dev_core) for k in range(CHUNKS)]
@@ -147,9 +143,11 @@
     r1m, r1 = first_copies(R, dev_za)
 
     pl.semaphore_wait(barrier, 7)
-    start(r0m, c1m)
+    start(r0m, *r0, c1m)
     for k in range(CHUNKS):
-        start(r0[k], c1[k])
+        pack_column(ranked_columns[2], k, C.send[k], 0)
+        pack_column(ranked_columns[3], k, C.send[k], CAP)
+        start(c1[k])
     for k in range(CHUNKS):
         pack_column(ranked_columns[0], k, C.first[k], 0)
         pack_column(ranked_columns[1], k, C.first[k], CAP)
@@ -174,7 +172,7 @@
             dst[first + j] = jnp.where(j < count, block, zero)
 
     landed(r0m)
-    ranked_rows = [rank_row(role, q) for role, q in enumerate((z, zb, za, zd))]
+    ranked_rows = {role: rank_row(role, q) for role, q in ((2, za), (3, zd))}
     start(r1m)
     for k in range(CHUNKS):
         landed(r0[k])
@@ -288,15 +286,19 @@
         if i < 6:
             start(trace[i + 1])
 
-    for k in each:
-        pack_row(ranked_rows[0], k, R.first[k], 0)
-        pack_row(ranked_rows[1], k, R.first[k], CAP)
-    total = jnp.zeros((8, BS), jnp.float32)
-    for k in each:
-        total = total + squares(C.send[k])
-        total = total + squares(C.first[k])
-    tacc[0] = total
-    start(trace[0])
+    def own_rows():
+        ranked_rows.update({role: rank_row(role, q) for role, q in ((0, z), (1, zb))})
+        for k in each:
+            pack_row(ranked_rows[0], k, R.first[k], 0)
+            pack_row(ranked_rows[1], k, R.first[k], CAP)
+
+    def begin_trace():
+        total = jnp.zeros((8, BS), jnp.float32)
+        for k in each:
+            total = total + squares(C.send[k])
+            total = total + squares(C.first[k])
+        tacc[0] = total
+        start(trace[0])
 
     def match(row_role, carry):
         have = [R.l_final[row_role * LIST + 1 + i] for i in range(CAP)]
@@ -335,9 +337,11 @@
         ]
     steps += [
         (0.9, lambda: lists1(C, c1m, c2m, IX_C1B, IX_C1O)),
+        (1.05, lambda: own_rows()),
         (1.1, lambda: lists1(R, r1m, r2m, IX_R1B, IX_R1O)),
+        (1.76, lambda: begin_trace()),
         (1.3, lambda: lists2(C, c2m, c3m, IX_C2)),
-        (1.8, lambda: trace_step(0)),
+        (2.05, lambda: trace_step(0)),
         (2.1, lambda: lists2(R, r2m, r3m, IX_R2)),
         (2.2, lambda: lists3(C, c3m, (c4bm, c4am), IX_C3)),
         (2.9, lambda: lists3(R, r3m, (r4bm, r4am), IX_R3)),

time: 43.2 us -> 43.1 us (level)
  no operation moved by 1% of the time
where the time goes in v6:
time: 43.1 us; the launch traced here: 42.9 us
  Pallas kernels  38.9 us (90%)
  between operations  2.4 us (6%)
  local copies, waits for them, and re-layouts  1.65 us (4%)
    pallas_call x1, Pallas kernels, on_device(): pl.pallas_call(kernel, out_shape=(jax.ShapeDtypeStruct((8, BS, 4 * BS), j...  38.9 us
    unnamed x7, local copies, waits for them, and re-layouts  1.65 us

profile of v6, /device:TPU:1, one launch (start us, length us, event | category | flops | bytes accessed | tf_op | source)
XLA Modules:
  0.0 42.9 jit_solution(9136532798315821328)
XLA Ops:
  0.6 0.0 copy-start.1
  0.6 0.0 copy-start
  0.6 0.0 copy-start.2
  0.7 0.7 %copy-done.1 = s32[8,4]{0,1:T(4,128)S(1)} copy-done((s32[8,4]{0,1:T(4,128)S(1)}, s32[8,4]{0,1:T(4,128)}, u32[]{:S(2)}) %copy-start.1) | copy-done | bytes 152
  1.3 0.0 copy-done
  1.3 0.0 copy-done.2
  1.3 38.9 %shard_map.59 = (bf16[8,128,512]{2,1,0:T(8,128)(2,1)S(1)}, f32[1,1]{1,0:T(1,128)}) custom-call(bf16[8,128,512]{2,1,0:T(8,128)(2,1)} %bitcast.8, s32[4,8]{1,0:T(4,128)S(1)} %bitcast.6, s32[4,8]{1,0:T(4,128)S(1)} %bitcast.7, s32[64]{0:T(128)S(1)} %copy-done.2), custom_call_target="tpu_custom_call" | custom-call | flops 805306368 | bytes 4194304 | tf_op jit(solution)/shard_map/pallas_call | solution.py:416
  40.2 1.0 %copy.8 = bf16[1024,512]{1,0:T(8,128)(2,1)} copy(bf16[1024,512]{1,0:T(8,128)(2,1)S(1)} %bitcast.5) | data formatting | bytes 2097152
Async XLA Ops:
  0.6 0.7 %copy-start.1 = (s32[8,4]{0,1:T(4,128)S(1)}, s32[8,4]{0,1:T(4,128)}, u32[]{:S(2)}) copy-start(s32[8,4]{0,1:T(4,128)} %param.6) | copy-start | bytes 388
  0.6 0.7 %copy-start = (s32[8,4]{0,1:T(4,128)S(1)}, s32[8,4]{0,1:T(4,128)}, u32[]{:S(2)}) copy-start(s32[8,4]{0,1:T(4,128)} %param.5) | copy-start | bytes 388
  0.6 0.7 %copy-start.2 = (s32[64]{0:T(128)S(1)}, s32[64]{0:T(128)}, u32[]{:S(2)}) copy-start(s32[64]{0:T(128)} %assignment_in.1) | copy-start | bytes 772

commit v7 on v5

--- a/solution.py
+++ b/solution.py
@@ -317,6 +317,28 @@
         for one in copies:
             one.wait_send()
             done.append(one)
+
+    column_of = (x, xb, xa, xd)
+    line_by_role = (
+        [core * 4 + position for position in (z, zb, za, zd)]
+        + [(1 - core) * 4 + position for position in (z, za, zb, zd)]
+    )
+
+    def product(row_roles):
+        for c in range(4):
+            left = []
+            for role in row_roles:
+                base = IX_MATCH + (role * 4 + c) * CAP
+                left.append(jnp.concatenate([rows[role][table[base + j]] for j in range(CAP)], axis=1))
+            right = columns_panel[c * CAP:(c + 1) * CAP].reshape(CAP * BS, BS)
+            total = jnp.dot(
+                jnp.concatenate(left, axis=0), right, preferred_element_type=jnp.float32
+            )
+            q = column_of[c]
+            for i, role in enumerate(row_roles):
+                line = line_by_role[role]
+                kept = jnp.where(filter_mask[q, line] != 0, total[i * BS:(i + 1) * BS], 0.0)
+                out[line, :, pl.ds(pl.multiple_of(q * BS, BS), BS)] = kept.astype(jnp.bfloat16)
 
     row_lag = 0.75
     steps = []
@@ -352,40 +374,13 @@
         (5.1, lambda: trace_step(4)),
         (5.5, lambda: sent(c1m, *c1, r0m, *r0, r1m, *r1, c2m, *c2, r2m, *r2)),
         (5.85, lambda: trace_step(5)),
+        (6.3, lambda: (landed(*c4a, *c5), product((0, 1)))),
+        (6.4, lambda: (landed(*f[0], *f[1]), product((4, 5)))),
     ]
     for _, step in sorted(steps, key=lambda one: one[0]):
         step()
 
-    for k in each:
-        landed(c4a[k], c5[k])
-
-    column_of = (x, xb, xa, xd)
-    line_by_role = (
-        [core * 4 + position for position in (z, zb, za, zd)]
-        + [(1 - core) * 4 + position for position in (z, za, zb, zd)]
-    )
-
-    def product(row_roles):
-        for c in range(4):
-            left = []
-            for role in row_roles:
-                base = IX_MATCH + (role * 4 + c) * CAP
-                left.append(jnp.concatenate([rows[role][table[base + j]] for j in range(CAP)], axis=1))
-            right = columns_panel[c * CAP:(c + 1) * CAP].reshape(CAP * BS, BS)
-            total = jnp.dot(
-                jnp.concatenate(left, axis=0), right, preferred_element_type=jnp.float32
-            )
-            q = column_of[c]
-            for i, role in enumerate(row_roles):
-                line = line_by_role[role]
-                kept = jnp.where(filter_mask[q, line] != 0, total[i * BS:(i + 1) * BS], 0.0)
-                out[line, :, pl.ds(pl.multiple_of(q * BS, BS), BS)] = kept.astype(jnp.bfloat16)
-
-    product((0, 1))
     product((2, 3))
-    for role in (0, 1):
-        landed(*f[role])
-    product((4, 5))
     sent(c3m, *c3, r3m, *r3, c4am, c4bm, r4am, r4bm, c5m, r5m, fm, *c4b, *trace[:5])
     for role in (2, 3):
         landed(*f[role])

time: 43.2 us -> 44.1 us (1.021)
  Pallas kernels: 39 us -> 39.9 us
    pallas_call x1, Pallas kernels: 39 us -> 39.9 us  [on_device(): pl.pallas_call(kernel, out_shape=(jax.ShapeDtypeStruct((8, BS, 4 * BS), j...]
where the time goes in v7:
time: 44.1 us; the launch traced here: 43.9 us
  Pallas kernels  39.9 us (90%)
  between operations  2.4 us (5%)
  local copies, waits for them, and re-layouts  1.65 us (4%)
    pallas_call x1, Pallas kernels, on_device(): pl.pallas_call(kernel, out_shape=(jax.ShapeDtypeStruct((8, BS, 4 * BS), j...  39.9 us
    unnamed x7, local copies, waits for them, and re-layouts  1.65 us

profile of v7, /device:TPU:1, one launch (start us, length us, event | category | flops | bytes accessed | tf_op | source)
XLA Modules:
  0.0 43.9 jit_solution(15768679433445184484)
XLA Ops:
  0.6 0.0 copy-start.1
  0.6 0.0 copy-start
  0.6 0.0 copy-start.2
  0.7 0.7 %copy-done.1 = s32[8,4]{0,1:T(4,128)S(1)} copy-done((s32[8,4]{0,1:T(4,128)S(1)}, s32[8,4]{0,1:T(4,128)}, u32[]{:S(2)}) %copy-start.1) | copy-done | bytes 152
  1.3 0.0 copy-done
  1.3 0.0 copy-done.2
  1.3 39.9 %shard_map.59 = (bf16[8,128,512]{2,1,0:T(8,128)(2,1)S(1)}, f32[1,1]{1,0:T(1,128)}) custom-call(bf16[8,128,512]{2,1,0:T(8,128)(2,1)} %bitcast.8, s32[4,8]{1,0:T(4,128)S(1)} %bitcast.6, s32[4,8]{1,0:T(4,128)S(1)} %bitcast.7, s32[64]{0:T(128)S(1)} %copy-done.2), custom_call_target="tpu_custom_call" | custom-call | flops 805306368 | bytes 4194304 | tf_op jit(solution)/shard_map/pallas_call | solution.py:407
  41.2 1.0 %copy.8 = bf16[1024,512]{1,0:T(8,128)(2,1)} copy(bf16[1024,512]{1,0:T(8,128)(2,1)S(1)} %bitcast.5) | data formatting | bytes 2097152
Async XLA Ops:
  0.6 0.7 %copy-start.1 = (s32[8,4]{0,1:T(4,128)S(1)}, s32[8,4]{0,1:T(4,128)}, u32[]{:S(2)}) copy-start(s32[8,4]{0,1:T(4,128)} %param.6) | copy-start | bytes 388
  0.6 0.7 %copy-start = (s32[8,4]{0,1:T(4,128)S(1)}, s32[8,4]{0,1:T(4,128)}, u32[]{:S(2)}) copy-start(s32[8,4]{0,1:T(4,128)} %param.5) | copy-start | bytes 388
  0.6 0.7 %copy-start.2 = (s32[64]{0:T(128)S(1)}, s32[64]{0:T(128)}, u32[]{:S(2)}) copy-start(s32[64]{0:T(128)} %assignment_in.1) | copy-start | bytes 772

commit v8 on v5

--- a/solution.py
+++ b/solution.py
@@ -356,17 +356,14 @@
     for _, step in sorted(steps, key=lambda one: one[0]):
         step()
 
-    for k in each:
-        landed(c4a[k], c5[k])
-
     column_of = (x, xb, xa, xd)
     line_by_role = (
         [core * 4 + position for position in (z, zb, za, zd)]
         + [(1 - core) * 4 + position for position in (z, za, zb, zd)]
     )
 
-    def product(row_roles):
-        for c in range(4):
+    def product(row_roles, column_roles):
+        for c in column_roles:
             left = []
             for role in row_roles:
                 base = IX_MATCH + (role * 4 + c) * CAP
@@ -381,18 +378,21 @@
                 kept = jnp.where(filter_mask[q, line] != 0, total[i * BS:(i + 1) * BS], 0.0)
                 out[line, :, pl.ds(pl.multiple_of(q * BS, BS), BS)] = kept.astype(jnp.bfloat16)
 
-    product((0, 1))
-    product((2, 3))
-    for role in (0, 1):
-        landed(*f[role])
-    product((4, 5))
+    first_three = (0, 1, 2)
+    landed(*c4a)
+    product((0, 1), first_three)
+    product((2, 3), first_three)
+    landed(*f[0], *f[1])
+    product((4, 5), first_three)
     sent(c3m, *c3, r3m, *r3, c4am, c4bm, r4am, r4bm, c5m, r5m, fm, *c4b, *trace[:5])
-    for role in (2, 3):
-        landed(*f[role])
-    product((6, 7))
-
+    landed(*f[2], *f[3])
+    product((6, 7), first_three)
     trace_step(6)
     occupation[0, 0] = jnp.sum(tacc[7])
+    landed(*c5)
+    product((0, 1, 2, 3), (3,))
+    product((4, 5, 6, 7), (3,))
+
     for one in remote:
         if not any(one is other_one for other_one in done):
             one.wait_send()

time: 43.2 us -> 43.7 us (1.012)
  Pallas kernels: 39 us -> 39.5 us
    pallas_call x1, Pallas kernels: 39 us -> 39.5 us  [on_device(): pl.pallas_call(kernel, out_shape=(jax.ShapeDtypeStruct((8, BS, 4 * BS), j...]
where the time goes in v8:
time: 43.7 us; the launch traced here: 43.5 us
  Pallas kernels  39.5 us (90%)
  between operations  2.4 us (5%)
  local copies, waits for them, and re-layouts  1.65 us (4%)
    pallas_call x1, Pallas kernels, on_device(): pl.pallas_call(kernel, out_shape=(jax.ShapeDtypeStruct((8, BS, 4 * BS), j...  39.5 us
    unnamed x7, local copies, waits for them, and re-layouts  1.65 us

profile of v8, /device:TPU:1, one launch (start us, length us, event | category | flops | bytes accessed | tf_op | source)
XLA Modules:
  0.0 43.5 jit_solution(6735239846396600199)
XLA Ops:
  0.6 0.0 copy-start.1
  0.6 0.0 copy-start
  0.6 0.0 copy-start.2
  0.7 0.7 %copy-done.1 = s32[8,4]{0,1:T(4,128)S(1)} copy-done((s32[8,4]{0,1:T(4,128)S(1)}, s32[8,4]{0,1:T(4,128)}, u32[]{:S(2)}) %copy-start.1) | copy-done | bytes 152
  1.3 0.0 copy-done
  1.3 0.0 copy-done.2
  1.3 39.5 %shard_map.59 = (bf16[8,128,512]{2,1,0:T(8,128)(2,1)S(1)}, f32[1,1]{1,0:T(1,128)}) custom-call(bf16[8,128,512]{2,1,0:T(8,128)(2,1)} %bitcast.8, s32[4,8]{1,0:T(4,128)S(1)} %bitcast.6, s32[4,8]{1,0:T(4,128)S(1)} %bitcast.7, s32[64]{0:T(128)S(1)} %copy-done.2), custom_call_target="tpu_custom_call" | custom-call | flops 805306368 | bytes 4194304 | tf_op jit(solution)/shard_map/pallas_call | solution.py:412
  40.8 1.0 %copy.8 = bf16[1024,512]{1,0:T(8,128)(2,1)} copy(bf16[1024,512]{1,0:T(8,128)(2,1)S(1)} %bitcast.5) | data formatting | bytes 2097152
Async XLA Ops:
  0.6 0.7 %copy-start.1 = (s32[8,4]{0,1:T(4,128)S(1)}, s32[8,4]{0,1:T(4,128)}, u32[]{:S(2)}) copy-start(s32[8,4]{0,1:T(4,128)} %param.6) | copy-start | bytes 388
  0.6 0.7 %copy-start = (s32[8,4]{0,1:T(4,128)S(1)}, s32[8,4]{0,1:T(4,128)}, u32[]{:S(2)}) copy-start(s32[8,4]{0,1:T(4,128)} %param.5) | copy-start | bytes 388
  0.6 0.7 %copy-start.2 = (s32[64]{0:T(128)S(1)}, s32[64]{0:T(128)}, u32[]{:S(2)}) copy-start(s32[64]{0:T(128)} %assignment_in.1) | copy-start | bytes 772

commit v9 on v5

--- a/solution.py
+++ b/solution.py
@@ -318,20 +318,20 @@
             one.wait_send()
             done.append(one)
 
-    row_lag = 0.75
+    row_lag, gap = 0.75, 0.9
     steps = []
     for k in each:
         steps += [
-            (1 + k, lambda k=k: blocks1(C, c1, c2, IX_C1B, IX_C1O, k)),
-            (2 + k, lambda k=k: blocks2(C, c2, c3, IX_C2, k)),
-            (3 + k, lambda k=k: blocks3_column(k)),
-            (4 + k, lambda k=k: (landed(c4b[k]), start(c5[k]))),
-            (1 + k + row_lag, lambda k=k: blocks1(R, r1, r2, IX_R1B, IX_R1O, k)),
-            (2 + k + row_lag, lambda k=k: blocks2(R, r2, r3, IX_R2, k)),
-            (3 + k + row_lag, lambda k=k: blocks3_row(k)),
-            (4 + k + row_lag, lambda k=k: (landed(r4b[k]), start(r5[k], f[1][k]))),
-            (4.2 + k + row_lag, lambda k=k: (landed(r4a[k]), start(f[2][k]))),
-            (5 + k + row_lag, lambda k=k: (landed(r5[k]), start(f[3][k]))),
+            (1 + gap * k, lambda k=k: blocks1(C, c1, c2, IX_C1B, IX_C1O, k)),
+            (2 + gap * k, lambda k=k: blocks2(C, c2, c3, IX_C2, k)),
+            (3 + gap * k, lambda k=k: blocks3_column(k)),
+            (4 + gap * k, lambda k=k: (landed(c4b[k]), start(c5[k]))),
+            (1 + gap * k + row_lag, lambda k=k: blocks1(R, r1, r2, IX_R1B, IX_R1O, k)),
+            (2 + gap * k + row_lag, lambda k=k: blocks2(R, r2, r3, IX_R2, k)),
+            (3 + gap * k + row_lag, lambda k=k: blocks3_row(k)),
+            (4 + gap * k + row_lag, lambda k=k: (landed(r4b[k]), start(r5[k], f[1][k]))),
+            (4.2 + gap * k + row_lag, lambda k=k: (landed(r4a[k]), start(f[2][k]))),
+            (5 + gap * k + row_lag, lambda k=k: (landed(r5[k]), start(f[3][k]))),
         ]
     steps += [
         (0.9, lambda: lists1(C, c1m, c2m, IX_C1B, IX_C1O)),

time: 43.2 us -> 44.4 us (1.028)
  Pallas kernels: 39 us -> 40.2 us
    pallas_call x1, Pallas kernels: 39 us -> 40.2 us  [on_device(): pl.pallas_call(kernel, out_shape=(jax.ShapeDtypeStruct((8, BS, 4 * BS), j...]
where the time goes in v9:
time: 44.4 us; the launch traced here: 44.2 us
  Pallas kernels  40.2 us (91%)
  between operations  2.4 us (5%)
  local copies, waits for them, and re-layouts  1.65 us (4%)
    pallas_call x1, Pallas kernels, on_device(): pl.pallas_call(kernel, out_shape=(jax.ShapeDtypeStruct((8, BS, 4 * BS), j...  40.2 us
    unnamed x7, local copies, waits for them, and re-layouts  1.65 us

profile of v9, /device:TPU:1, one launch (start us, length us, event | category | flops | bytes accessed | tf_op | source)
XLA Modules:
  0.0 44.2 jit_solution(3693164419916228772)
XLA Ops:
  0.6 0.0 copy-start.1
  0.6 0.0 copy-start
  0.6 0.0 copy-start.2
  0.7 0.7 %copy-done.1 = s32[8,4]{0,1:T(4,128)S(1)} copy-done((s32[8,4]{0,1:T(4,128)S(1)}, s32[8,4]{0,1:T(4,128)}, u32[]{:S(2)}) %copy-start.1) | copy-done | bytes 152
  1.3 0.0 copy-done
  1.3 0.0 copy-done.2
  1.3 40.2 %shard_map.59 = (bf16[8,128,512]{2,1,0:T(8,128)(2,1)S(1)}, f32[1,1]{1,0:T(1,128)}) custom-call(bf16[8,128,512]{2,1,0:T(8,128)(2,1)} %bitcast.8, s32[4,8]{1,0:T(4,128)S(1)} %bitcast.6, s32[4,8]{1,0:T(4,128)S(1)} %bitcast.7, s32[64]{0:T(128)S(1)} %copy-done.2), custom_call_target="tpu_custom_call" | custom-call | flops 805306368 | bytes 4194304 | tf_op jit(solution)/shard_map/pallas_call | solution.py:412
  41.5 1.0 %copy.8 = bf16[1024,512]{1,0:T(8,128)(2,1)} copy(bf16[1024,512]{1,0:T(8,128)(2,1)S(1)} %bitcast.5) | data formatting | bytes 2097152
Async XLA Ops:
  0.6 0.7 %copy-start.1 = (s32[8,4]{0,1:T(4,128)S(1)}, s32[8,4]{0,1:T(4,128)}, u32[]{:S(2)}) copy-start(s32[8,4]{0,1:T(4,128)} %param.6) | copy-start | bytes 388
  0.6 0.7 %copy-start = (s32[8,4]{0,1:T(4,128)S(1)}, s32[8,4]{0,1:T(4,128)}, u32[]{:S(2)}) copy-start(s32[8,4]{0,1:T(4,128)} %param.5) | copy-start | bytes 388
  0.6 0.7 %copy-start.2 = (s32[64]{0:T(128)S(1)}, s32[64]{0:T(128)}, u32[]{:S(2)}) copy-start(s32[64]{0:T(128)} %assignment_in.1) | copy-start | bytes 772

commit v10 on v5

--- a/solution.py
+++ b/solution.py
@@ -40,14 +40,14 @@
     x, y_hi = row // 2, row % 2
     y_lo, z, core = col // 8, (col // 2) % 4, col % 2
 
-    def partners(position):
+    def partners(position, core):
         even, odd = position + 1 - 2 * (position % 2), 3 - position
         a = even * (1 - core) + odd * core
         b = odd * (1 - core) + even * core
         return a, b, (position + 2) % 4
 
-    xa, xb, xd = partners(x)
-    za, zb, zd = partners(z)
+    xa, xb, xd = partners(x, core)
+    za, zb, zd = partners(z, 1 - core)
     dev_xa, dev_xb = (xa * 2 + y_hi, col), (xb * 2 + y_hi, col)
     dev_yh = (x * 2 + 1 - y_hi, col)
     dev_za = (row, y_lo * 8 + za * 2 + core)

time: 43.2 us -> 44.4 us (1.028)
  Pallas kernels: 39 us -> 40.1 us
    pallas_call x1, Pallas kernels: 39 us -> 40.1 us  [on_device(): pl.pallas_call(kernel, out_shape=(jax.ShapeDtypeStruct((8, BS, 4 * BS), j...]
where the time goes in v10:
time: 44.4 us; the launch traced here: 44.2 us
  Pallas kernels  40.1 us (90%)
  between operations  2.4 us (5%)
  local copies, waits for them, and re-layouts  1.65 us (4%)
    pallas_call x1, Pallas kernels, on_device(): pl.pallas_call(kernel, out_shape=(jax.ShapeDtypeStruct((8, BS, 4 * BS), j...  40.1 us
    unnamed x7, local copies, waits for them, and re-layouts  1.65 us

profile of v10, /device:TPU:1, one launch (start us, length us, event | category | flops | bytes accessed | tf_op | source)
XLA Modules:
  0.0 44.2 jit_solution(5819891678508340950)
XLA Ops:
  0.6 0.0 copy-start.1
  0.6 0.0 copy-start
  0.6 0.0 copy-start.2
  0.7 0.7 %copy-done.1 = s32[8,4]{0,1:T(4,128)S(1)} copy-done((s32[8,4]{0,1:T(4,128)S(1)}, s32[8,4]{0,1:T(4,128)}, u32[]{:S(2)}) %copy-start.1) | copy-done | bytes 152
  1.3 0.0 copy-done
  1.3 0.0 copy-done.2
  1.3 40.1 %shard_map.59 = (bf16[8,128,512]{2,1,0:T(8,128)(2,1)S(1)}, f32[1,1]{1,0:T(1,128)}) custom-call(bf16[8,128,512]{2,1,0:T(8,128)(2,1)} %bitcast.8, s32[4,8]{1,0:T(4,128)S(1)} %bitcast.6, s32[4,8]{1,0:T(4,128)S(1)} %bitcast.7, s32[64]{0:T(128)S(1)} %copy-done.2), custom_call_target="tpu_custom_call" | custom-call | flops 805306368 | bytes 4194304 | tf_op jit(solution)/shard_map/pallas_call | solution.py:412
  41.5 1.0 %copy.8 = bf16[1024,512]{1,0:T(8,128)(2,1)} copy(bf16[1024,512]{1,0:T(8,128)(2,1)S(1)} %bitcast.5) | data formatting | bytes 2097152
Async XLA Ops:
  0.6 0.7 %copy-start.1 = (s32[8,4]{0,1:T(4,128)S(1)}, s32[8,4]{0,1:T(4,128)}, u32[]{:S(2)}) copy-start(s32[8,4]{0,1:T(4,128)} %param.6) | copy-start | bytes 388
  0.6 0.7 %copy-start = (s32[8,4]{0,1:T(4,128)S(1)}, s32[8,4]{0,1:T(4,128)}, u32[]{:S(2)}) copy-start(s32[8,4]{0,1:T(4,128)} %param.5) | copy-start | bytes 388
  0.6 0.7 %copy-start.2 = (s32[64]{0:T(128)S(1)}, s32[64]{0:T(128)}, u32[]{:S(2)}) copy-start(s32[64]{0:T(128)} %assignment_in.1) | copy-start | bytes 772

commit v11 on v5

--- a/solution.py
+++ b/solution.py
@@ -149,7 +149,7 @@
     pl.semaphore_wait(barrier, 7)
     start(r0m, c1m)
     for k in range(CHUNKS):
-        start(r0[k], c1[k])
+        start(c1[k], r0[k])
     for k in range(CHUNKS):
         pack_column(ranked_columns[0], k, C.first[k], 0)
         pack_column(ranked_columns[1], k, C.first[k], CAP)

time: 43.2 us -> 43.2 us (level)
  no operation moved by 1% of the time
where the time goes in v11:
time: 43.2 us; the launch traced here: 43 us
  Pallas kernels  39 us (90%)
  between operations  2.4 us (6%)
  local copies, waits for them, and re-layouts  1.65 us (4%)
    pallas_call x1, Pallas kernels, on_device(): pl.pallas_call(kernel, out_shape=(jax.ShapeDtypeStruct((8, BS, 4 * BS), j...  39 us
    unnamed x7, local copies, waits for them, and re-layouts  1.65 us

profile of v11, /device:TPU:1, one launch (start us, length us, event | category | flops | bytes accessed | tf_op | source)
XLA Modules:
  0.0 43.0 jit_solution(14575315408826588599)
XLA Ops:
  0.6 0.0 copy-start.1
  0.6 0.0 copy-start
  0.6 0.0 copy-start.2
  0.7 0.7 %copy-done.1 = s32[8,4]{0,1:T(4,128)S(1)} copy-done((s32[8,4]{0,1:T(4,128)S(1)}, s32[8,4]{0,1:T(4,128)}, u32[]{:S(2)}) %copy-start.1) | copy-done | bytes 152
  1.3 0.0 copy-done
  1.3 0.0 copy-done.2
  1.3 39.0 %shard_map.59 = (bf16[8,128,512]{2,1,0:T(8,128)(2,1)S(1)}, f32[1,1]{1,0:T(1,128)}) custom-call(bf16[8,128,512]{2,1,0:T(8,128)(2,1)} %bitcast.8, s32[4,8]{1,0:T(4,128)S(1)} %bitcast.6, s32[4,8]{1,0:T(4,128)S(1)} %bitcast.7, s32[64]{0:T(128)S(1)} %copy-done.2), custom_call_target="tpu_custom_call" | custom-call | flops 805306368 | bytes 4194304 | tf_op jit(solution)/shard_map/pallas_call | solution.py:412
  40.3 1.0 %copy.8 = bf16[1024,512]{1,0:T(8,128)(2,1)} copy(bf16[1024,512]{1,0:T(8,128)(2,1)S(1)} %bitcast.5) | data formatting | bytes 2097152
Async XLA Ops:
  0.6 0.7 %copy-start.1 = (s32[8,4]{0,1:T(4,128)S(1)}, s32[8,4]{0,1:T(4,128)}, u32[]{:S(2)}) copy-start(s32[8,4]{0,1:T(4,128)} %param.6) | copy-start | bytes 388
  0.6 0.7 %copy-start = (s32[8,4]{0,1:T(4,128)S(1)}, s32[8,4]{0,1:T(4,128)}, u32[]{:S(2)}) copy-start(s32[8,4]{0,1:T(4,128)} %param.5) | copy-start | bytes 388
  0.6 0.7 %copy-start.2 = (s32[64]{0:T(128)S(1)}, s32[64]{0:T(128)}, u32[]{:S(2)}) copy-start(s32[64]{0:T(128)} %assignment_in.1) | copy-start | bytes 772
